TPU v7x, 128 devices: a whole 4x4x4 slice. The times are simulated.
128 devices in a mesh: row: 8 (over x, core), col: 16 (over y, z).
Axes of the slice: x: 4, y: 4, z: 4, core: 2. Of those that a mesh axis runs over, the one named last changes fastest.
Arguments:
- hamiltonian: bfloat16 [5824, 5824], P('row', 'col'), may hold values from -6 to 6
- new_atom: int32 [448], replicated, may hold values from 0 to 447, as said below
- pattern: int32 [448, 448], P('row', 'col'), may hold values 0 or 1
Outputs:
- sign_matrix: float32 [5824, 5824], P('row', 'col')
Inputs may be any that keep to these rules, and one draw needn't show every extreme that they name: `new_atom`: each old atom appears once. Block column b holds atoms b * 28 to (b + 1) * 28 - 1 in both orders. For each new block column d and each v from 0 to 27, exactly one atom of new block column d comes from old block column (d - 1 - (v mod 16)) mod 16, so the number of atoms that old block column b sends to new block column (b + k) mod 16 is the number of such v with (1 + v) mod 16 = k.
All inputs are finite; a program needn't handle non-finite values. No bound on the sum of `pattern` on one device may be relied on, other than what follows from the above.
Results may differ from a plain program's by a relative error of at most 0.0029.
Values may be sent and summed in bfloat16 or wider, within the bound.
No kernel may reach another device: no remote copies, remote signals or barrier semaphores. Data moves between devices by JAX's collectives and lax.ppermute only.
A program may use at most 64 MiB of HBM per device.

v0:
```python
import functools
import jax
import jax.numpy as jnp
import numpy as np
from jax import lax
from jax.sharding import Mesh
from jax.sharding import PartitionSpec as P

NBF = 13
ROW = ("row_0", "row_1")
COL = ("col_0", "col_1")
ROW_COL = ("row_0", "row_1", "col_0", "col_1")


def by_axis(array, axes):
    return functools.reduce(lax.psum, axes, array)


def expand(atoms):
    return (atoms[:, None] * NBF + jnp.arange(NBF, dtype=jnp.int32)[None, :]).reshape(-1)


def pack_slots(new_atom, here, per_block, groups, slots):
    source = new_atom.reshape(groups, per_block) // per_block
    local = new_atom.reshape(groups, per_block) - here * per_block
    mine = source == here
    rank = jnp.cumsum(mine.astype(jnp.int32), axis=1) - 1
    number = jnp.arange(slots, dtype=jnp.int32)
    hit = mine[:, None, :] & (rank[:, None, :] == number[None, :, None])
    atoms = jnp.sum(jnp.where(hit, local[:, None, :], 0), axis=2)
    used = jnp.any(hit, axis=2)
    return (atoms.reshape(-1), jnp.repeat(used.reshape(-1), NBF))


def place_slots(new_atom, here, per_block, groups, slots):
    source = lax.dynamic_slice_in_dim(new_atom, here * per_block, per_block) // per_block
    onehot = source[:, None] == jnp.arange(groups, dtype=jnp.int32)[None, :]
    running = jnp.cumsum(onehot.astype(jnp.int32), axis=0) - 1
    rank = jnp.sum(jnp.where(onehot, running, 0), axis=1)
    return expand((source * slots + rank).astype(jnp.int32))


def fold_right(row_panel, right):
    return jnp.dot(
        row_panel,
        lax.all_gather(right, ROW, axis=0, tiled=True),
        preferred_element_type=jnp.float32,
    )


def on_device(hamiltonian, new_atom, pattern):
    rows_here, cols_here = hamiltonian.shape
    row_count = lax.axis_size(ROW)
    col_count = lax.axis_size(COL)
    order_all = rows_here * row_count
    atoms_row = rows_here // NBF
    atoms_col = cols_here // NBF
    ratio = col_count // row_count
    counts = np.bincount((1 + np.arange(atoms_col)) % col_count, minlength=col_count)
    targets = (np.arange(ratio)[:, None] + np.arange(col_count)[None, :]) % col_count // ratio
    per_target = np.sum(
        (targets[None, :, :] == np.arange(row_count)[:, None, None]) * counts[None, None, :],
        axis=(1, 2),
    )
    slots_row = max(int(np.max(per_target)), 1)
    slots_col = max(int(np.max(counts)), 1)
    row_here = lax.axis_index(ROW)
    col_here = lax.axis_index(COL)
    atoms, flags = pack_slots(new_atom, row_here, atoms_row, row_count, slots_row)
    outgoing = jnp.where(
        flags[:, None], jnp.take(hamiltonian, expand(atoms), axis=0), jnp.zeros((), jnp.bfloat16)
    )
    arrived = lax.all_to_all(outgoing, ROW, split_axis=0, concat_axis=0, tiled=True)
    moved = jnp.take(
        arrived, place_slots(new_atom, row_here, atoms_row, row_count, slots_row), axis=0
    )
    atoms, flags = pack_slots(new_atom, col_here, atoms_col, col_count, slots_col)
    outgoing = jnp.where(
        flags[None, :], jnp.take(moved, expand(atoms), axis=1), jnp.zeros((), jnp.bfloat16)
    )
    arrived = lax.all_to_all(outgoing, COL, split_axis=1, concat_axis=1, tiled=True)
    moved = jnp.take(
        arrived, place_slots(new_atom, col_here, atoms_col, col_count, slots_col), axis=1
    )
    atom_rows, atom_cols = pattern.shape
    keep = jnp.broadcast_to(
        pattern.astype(jnp.float32)[:, None, :, None], (atom_rows, NBF, atom_cols, NBF)
    ).reshape(rows_here, cols_here)
    masked = moved.astype(jnp.float32) * keep
    total = by_axis(jnp.sum(masked * masked), ROW_COL)
    start = (masked * lax.rsqrt(total / order_all)).astype(jnp.bfloat16)
    kept = lax.all_gather(start, COL, axis=1, tiled=True)
    square = (fold_right(kept, start) * keep).astype(jnp.bfloat16)
    cube = fold_right(kept, square) * keep
    return keep * (1.5 * start.astype(jnp.float32) - 0.5 * cube)


def solution(mesh):
    split = Mesh(mesh.devices.reshape(4, 2, 4, 4), ("row_0", "row_1", "col_0", "col_1"))
    in_specs = (P(ROW, COL), P(), P(ROW, COL))
    out_specs = P(ROW, COL)
    return jax.shard_map(
        on_device, mesh=split, in_specs=in_specs, out_specs=out_specs, check_vma=False
    )
```

profile of v0, /device:TPU:1, one launch (start us, length us, event | category | flops | bytes accessed | tf_op | source)
XLA Modules:
  0.0 264.0 jit_solution(595021071242153486)
XLA Ops:
  9.7 3.5 %gather_fusion = bf16[832,364]{1,0:T(8,128)(2,1)S(1)} fusion(bf16[728,364]{1,0:T(8,128)(2,1)S(1)} %copy-done, s32[1024]{0:T(1024)S(1)} %pad_clamp_fusion.3), kind=kCustom, calls=%fused_computation | custom fusion | bytes 1214720 | tf_op jit(solution)/shard_map/jit(_take)/gather | solution.py:71
  13.2 1.1 select_select_fusion.1
  14.4 5.8 %all-to-all-start = ((bf16[8,104,364]{2,1,0:T(8,128)(2,1)}), bf16[8,104,364]{2,1,0:T(8,128)(2,1)S(1)}, u32[]{:S(2)}, u32[]{:S(2)}) async-start(bf16[8,104,364]{2,1,0:T(8,128)(2,1)} %select_select_fusion.1), calls=%async_computation | async-start | bytes 1277952 | tf_op jit(solution)/shard_map/all_to_all | solution.py:73
  23.1 7.8 %all-to-all-done = bf16[8,104,364]{2,1,0:T(8,128)(2,1)S(1)} async-done(((bf16[8,104,364]{2,1,0:T(8,128)(2,1)}), bf16[8,104,364]{2,1,0:T(8,128)(2,1)S(1)}, u32[]{:S(2)}, u32[]{:S(2)}) %all-to-all-start) | async-done | bytes 605728 | tf_op jit(solution)/shard_map/all_to_all | solution.py:73
  30.9 3.0 %gather_fusion.1 = bf16[728,364]{1,0:T(8,128)(2,1)S(1)} fusion(bf16[832,364]{1,0:T(8,128)(2,1)S(1)} %bitcast.35, s32[1024]{0:T(1024)S(1)} %pad_clamp_fusion.2), kind=kCustom, calls=%fused_computation.1 | custom fusion | bytes 1062880 | tf_op jit(solution)/shard_map/jit(_take)/gather | solution.py:74
  34.3 2.2 gather_fusion.2
  36.7 1.1 select_select_fusion
  37.8 7.9 %all-to-all-start.1 = ((bf16[728,16,26]{0,2,1:T(8,128)(2,1)}), bf16[728,16,26]{0,2,1:T(8,128)(2,1)}, u32[]{:S(2)}, u32[]{:S(2)}) async-start(bf16[728,16,26]{0,2,1:T(8,128)(2,1)} %select_select_fusion), calls=%async_computation.1 | async-start | bytes 1572864 | tf_op jit(solution)/shard_map/all_to_all | solution.py:81
  46.2 4.7 %broadcast_in_dim.132 = f32[56,13,28,13]{1,0,3,2:T(8,128)} broadcast(f32[56,28]{0,1:T(8,128)S(1)} %convert_element_type.41), dimensions={0,2} | broadcast | bytes 1066240 | tf_op jit(solution)/shard_map/broadcast_in_dim | solution.py:86
  50.9 6.7 %reshape.368 = f32[728,364]{0,1:T(8,128)S(1)} reshape(f32[56,13,28,13]{1,0,3,2:T(8,128)} %broadcast_in_dim.132) | data formatting | bytes 2119936 | tf_op jit(solution)/shard_map/reshape | solution.py:88
  58.5 1.5 all_to_all.15
  60.0 2.2 gather_fusion.3
  63.3 7.5 %psum.28 = f32[]{:T(128)} all-reduce(f32[]{:T(128)} %fusion.5), channel_id=1, replica_groups=mesh['row_0'=4,'row_1'=2,'col_0'=4,'col_1'=4] {'row_0'}, use_global_device_ids=true, to_apply=%region_11.12 | all-reduce | flops 1 | bytes 8 | tf_op jit(solution)/shard_map/psum | solution.py:16
  70.8 7.3 %psum.29 = f32[]{:T(128)} all-reduce(f32[]{:T(128)} %psum.28), channel_id=1, replica_groups=mesh['row_0'=4,'row_1'=2,'col_0'=4,'col_1'=4] {'row_1'}, use_global_device_ids=true, to_apply=%region_12.13 | all-reduce | flops 1 | bytes 8 | tf_op jit(solution)/shard_map/psum | solution.py:16
  78.2 7.6 %psum.30 = f32[]{:T(128)} all-reduce(f32[]{:T(128)} %psum.29), channel_id=1, replica_groups=mesh['row_0'=4,'row_1'=2,'col_0'=4,'col_1'=4] {'col_0'}, use_global_device_ids=true, to_apply=%region_13.14 | all-reduce | flops 1 | bytes 8 | tf_op jit(solution)/shard_map/psum | solution.py:16
  85.8 9.0 %psum.31 = f32[]{:T(128)} all-reduce(f32[]{:T(128)} %psum.30), channel_id=1, replica_groups=mesh['row_0'=4,'row_1'=2,'col_0'=4,'col_1'=4] {'col_1'}, use_global_device_ids=true, to_apply=%region_14.15 | all-reduce | flops 1 | bytes 8 | tf_op jit(solution)/shard_map/psum | solution.py:16
  95.5 1.0 fusion.7
  97.5 71.0 %all-gather.9.cloned.1.call-done = bf16[16,364,728]{1,2,0:T(8,128)(2,1)} async-done(((bf16[1,364,728]{1,2,0:T(8,128)(2,1)}), bf16[16,364,728]{1,2,0:T(8,128)(2,1)}) %all-gather.9.cloned.1.call-update) | async-done | bytes 8479760 | tf_op jit(solution)/shard_map/all_gather | solution.py:92
  168.5 8.1 %copy.35 = bf16[16,364,728]{1,0,2:T(8,128)(2,1)} copy(bf16[16,364,728]{1,2,0:T(8,128)(2,1)} %all-gather.9.cloned.1.call-done) | data formatting | bytes 16959488 | tf_op jit(solution)/shard_map/all_gather | solution.py:92
  176.7 15.8 %reshape.402 = bf16[5824,728]{0,1:T(8,128)(2,1)} reshape(bf16[16,364,728]{1,0,2:T(8,128)(2,1)} %copy.35) | data formatting | bytes 16959488
  192.5 11.0 %all-gather.5.cloned.1.call-done = bf16[5824,364]{1,0:T(8,128)(2,1)} async-done(((bf16[728,364]{1,0:T(8,128)(2,1)}), bf16[5824,364]{1,0:T(8,128)(2,1)}) %all-gather.5.cloned.1.call-update) | async-done | bytes 4239888 | tf_op jit(solution)/shard_map/all_gather | solution.py:46
  203.5 10.2 %fusion.3 = bf16[728,364]{1,0:T(8,128)(2,1)} fusion(f32[728,364]{1,0:T(8,128)S(1)} %copy.38, bf16[5824,728]{0,1:T(8,128)(2,1)} %reshape.402, bf16[5824,364]{1,0:T(8,128)(2,1)} %all-gather.5.cloned.1.call-done), kind=kOutput, calls=%fused_computation.9 | convolution fusion | flops 3087156736 | bytes 14309568 | tf_op jit(solution)/shard_map/dot_general | solution.py:44
  213.7 33.4 %all-gather.7.cloned.1.call-done = bf16[5824,364]{1,0:T(8,128)(2,1)} async-done(((bf16[728,364]{1,0:T(8,128)(2,1)}), bf16[5824,364]{1,0:T(8,128)(2,1)}) %all-gather.7.cloned.1.call-update) | async-done | bytes 4239888 | tf_op jit(solution)/shard_map/all_gather | solution.py:46
  247.1 10.3 %fusion.2 = f32[728,364]{1,0:T(8,128)} fusion(f32[728,364]{1,0:T(8,128)S(1)} %copy.38, bf16[5824,728]{0,1:T(8,128)(2,1)} %reshape.402, bf16[5824,364]{1,0:T(8,128)(2,1)} %all-gather.7.cloned.1.call-done, bf16[728,364]{1,0:T(8,128)(2,1)S(1)} %copy-done.1), kind=kOutput, calls=%fused_computation.8 | convolution fusion | flops 3088216576 | bytes 15369536 | tf_op jit(solution)/shard_map/dot_general | solution.py:44
  (92 shorter events, 10.2 us)
Async XLA Ops:
  6.5 3.2 %copy-start = (bf16[728,364]{1,0:T(8,128)(2,1)S(1)}, bf16[728,364]{1,0:T(8,128)(2,1)}, u32[]{:S(2)}) copy-start(bf16[728,364]{1,0:T(8,128)(2,1)} %param.3) | copy-start | bytes 1589956
  13.2 6.9 %copy-start.3 = (s32[448]{0:T(512)S(1)}, s32[448]{0:T(512)}, u32[]{:S(2)}) copy-start(s32[448]{0:T(512)} %param.4) | copy-start | bytes 5380
  14.4 16.5 %all-to-all-start = ((bf16[8,104,364]{2,1,0:T(8,128)(2,1)}), bf16[8,104,364]{2,1,0:T(8,128)(2,1)S(1)}, u32[]{:S(2)}, u32[]{:S(2)}) async-start(bf16[8,104,364]{2,1,0:T(8,128)(2,1)} %select_select_fusion.1), calls=%async_computation | async-start | bytes 1277952 | tf_op jit(solution)/shard_map/all_to_all | solution.py:73
  37.8 8.4 %copy-start.2 = (s32[56,28]{0,1:T(8,128)S(1)}, s32[56,28]{0,1:T(8,128)}, u32[]{:S(2)}) copy-start(s32[56,28]{0,1:T(8,128)} %param.5) | copy-start | bytes 18820
  37.8 20.8 %all-to-all-start.1 = ((bf16[728,16,26]{0,2,1:T(8,128)(2,1)}), bf16[728,16,26]{0,2,1:T(8,128)(2,1)}, u32[]{:S(2)}, u32[]{:S(2)}) async-start(bf16[728,16,26]{0,2,1:T(8,128)(2,1)} %select_select_fusion), calls=%async_computation.1 | async-start | bytes 1572864 | tf_op jit(solution)/shard_map/all_to_all | solution.py:81
  45.7 122.8 %all-gather.9.cloned.1.call-start = ((), (), s32[]{:S(2)}) async-start(), calls=%async_computation.4 | async-start | bytes 9504768 | tf_op jit(solution)/shard_map/all_gather | solution.py:92
  96.5 107.0 %all-gather.5.cloned.1.call-start = ((), (), s32[]{:S(2)}) async-start(), calls=%async_computation.2 | async-start | bytes 5031936 | tf_op jit(solution)/shard_map/all_gather | solution.py:46
  97.3 149.8 %all-gather.7.cloned.1.call-start = ((), (), s32[]{:S(2)}) async-start(), calls=%async_computation.3 | async-start | bytes 5031936 | tf_op jit(solution)/shard_map/all_gather | solution.py:46
  192.5 54.6 %copy-start.1 = (bf16[728,364]{1,0:T(8,128)(2,1)S(1)}, bf16[728,364]{1,0:T(8,128)(2,1)}, u32[]{:S(2)}) copy-start(bf16[728,364]{1,0:T(8,128)(2,1)} %fusion.7) | copy-start | bytes 1589956
Sparse Core Ops, SparseCore 0:
  96.7 71.8 all-gather.8
  170.2 33.2 all-gather.4
  213.8 33.2 all-gather.6
where the time goes:
time: 265 us; the launch traced here: 264 us
  waiting for transfers between devices  124 us (47%)
  local copies, waits for them, and re-layouts  51.2 us (19%)
  blocking collectives  31.4 us (12%)
  matrix products  20.5 us (8%)
  between operations  14.1 us (5%)
  starting transfers between devices  14 us (5%)
  other arithmetic  8.34 us (3%)
    all_gather x1, waiting for transfers between devices, on_device(): kept = lax.all_gather(start, COL, axis=1, tiled=True)  71 us
    all_gather x2, waiting for transfers between devices, fold_right(): lax.all_gather(right, ROW, axis=0, tiled=True)  44.4 us
    psum x4, blocking collectives, by_axis(): return functools.reduce(lax.psum, axes, array)  31.4 us
    dot_general x2, matrix products, fold_right(): jnp.dot(row_panel, lax.all_gather(right, ROW, axis=0, tiled=True), prefer...  20.5 us
    unnamed x9, local copies, waits for them, and re-layouts  15.9 us
    all_gather x1, local copies, waits for them, and re-layouts, on_device(): kept = lax.all_gather(start, COL, axis=1, tiled=True)  8.14 us
    all_to_all x1, starting transfers between devices, on_device(): lax.all_to_all(outgoing, COL, split_axis=1, concat_axis=1, tiled=True)  7.94 us
    all_to_all x1, waiting for transfers between devices, on_device(): lax.all_to_all(outgoing, ROW, split_axis=0, concat_axis=0, tiled=True)  7.77 us
  transfers between devices with their start and end apart: 5, of which 5 were waited for; matrix products, arithmetic and copies ran while one was open for 15% of the time, Pallas kernels for 0%

commit v1 on v0

--- a/solution.py
+++ b/solution.py
@@ -89,7 +89,10 @@
     masked = moved.astype(jnp.float32) * keep
     total = by_axis(jnp.sum(masked * masked), ROW_COL)
     start = (masked * lax.rsqrt(total / order_all)).astype(jnp.bfloat16)
-    kept = lax.all_gather(start, COL, axis=1, tiled=True)
+    kept = jnp.concatenate(
+        lax.all_to_all(jnp.stack([start for _ in range(lax.axis_size(COL))], axis=0), COL, 0, 0),
+        axis=1,
+    )
     square = (fold_right(kept, start) * keep).astype(jnp.bfloat16)
     cube = fold_right(kept, square) * keep
     return keep * (1.5 * start.astype(jnp.float32) - 0.5 * cube)

time: 265 us -> 318 us (1.20)
  waiting for transfers between devices: 124 us -> 169 us
  starting transfers between devices: 14 us -> 18.8 us
  local copies, waits for them, and re-layouts: 51.2 us -> 55.2 us
    all_to_all x0 -> x1, waiting for transfers between devices: none -> 118 us  [on_device(): lax.all_to_all(jnp.stack([start for _ in range(lax.axis_size(COL))], axis...]
    all_gather x1 -> x0, waiting for transfers between devices: 71 us -> none  [on_device(): kept = lax.all_gather(start, COL, axis=1, tiled=True)]
    reshape x0 -> x2, local copies, waits for them, and re-layouts: none -> 23.8 us  [on_device(): jnp.concatenate(lax.all_to_all(jnp.stack([start for _ in range(lax.axis_s...]
    unnamed x9 -> x12, local copies, waits for them, and re-layouts: 15.9 us -> 0.03 us
    all_gather x1 -> x0, local copies, waits for them, and re-layouts: 8.14 us -> none  [on_device(): kept = lax.all_gather(start, COL, axis=1, tiled=True)]
    all_to_all x0 -> x1, starting transfers between devices: none -> 4.75 us  [on_device(): lax.all_to_all(jnp.stack([start for _ in range(lax.axis_size(COL))], axis...]
    another operation x0 -> x1, local copies, waits for them, and re-layouts: none -> 4.22 us  [on_device(): jnp.stack([start for _ in range(lax.axis_size(COL))], axis=0)]
    all_gather x2, waiting for transfers between devices: 44.4 us -> 41.2 us  [fold_right(): lax.all_gather(right, ROW, axis=0, tiled=True)]
  transfers between devices with their start and end apart: 5 -> 5, of which waited for: 5 -> 4; matrix products, arithmetic and copies ran while one was open for 15% -> 12% of each run, Pallas kernels for 0% -> 0%
where the time goes in v1:
time: 318 us; the launch traced here: 317 us
  waiting for transfers between devices  169 us (53%)
  local copies, waits for them, and re-layouts  55.2 us (17%)
  blocking collectives  31.3 us (10%)
  matrix products  20.6 us (6%)
  starting transfers between devices  18.8 us (6%)
  between operations  14.5 us (5%)
  other arithmetic  7.54 us (2%)
    all_to_all x1, waiting for transfers between devices, on_device(): lax.all_to_all(jnp.stack([start for _ in range(lax.axis_size(COL))], axis...  118 us
    all_gather x2, waiting for transfers between devices, fold_right(): lax.all_gather(right, ROW, axis=0, tiled=True)  41.2 us
    psum x4, blocking collectives, by_axis(): return functools.reduce(lax.psum, axes, array)  31.3 us
    reshape x2, local copies, waits for them, and re-layouts, on_device(): jnp.concatenate(lax.all_to_all(jnp.stack([start for _ in range(lax.axis_s...  23.8 us
    dot_general x2, matrix products, fold_right(): jnp.dot(row_panel, lax.all_gather(right, ROW, axis=0, tiled=True), prefer...  20.6 us
    all_to_all x1, starting transfers between devices, on_device(): lax.all_to_all(outgoing, COL, split_axis=1, concat_axis=1, tiled=True)  7.94 us
    all_to_all x1, waiting for transfers between devices, on_device(): lax.all_to_all(outgoing, ROW, split_axis=0, concat_axis=0, tiled=True)  7.78 us
    reshape x2, local copies, waits for them, and re-layouts, on_device(): keep = jnp.broadcast_to(pattern.astype(jnp.float32)[:, None, :, None], (a...  7.1 us
  transfers between devices with their start and end apart: 5, of which 4 were waited for; matrix products, arithmetic and copies ran while one was open for 12% of the time, Pallas kernels for 0%

profile of v1, /device:TPU:1, one launch (start us, length us, event | category | flops | bytes accessed | tf_op | source)
XLA Modules:
  0.0 316.5 jit_solution(13466056134711212944)
XLA Ops:
  9.7 3.5 %gather_fusion = bf16[832,364]{1,0:T(8,128)(2,1)S(1)} fusion(bf16[728,364]{1,0:T(8,128)(2,1)S(1)} %copy-done, s32[1024]{0:T(1024)S(1)} %pad_clamp_fusion.3), kind=kCustom, calls=%fused_computation | custom fusion | bytes 1214720 | tf_op jit(solution)/shard_map/jit(_take)/gather | solution.py:71
  13.2 1.1 select_select_fusion.1
  14.4 5.8 %all-to-all-start = ((bf16[8,104,364]{2,1,0:T(8,128)(2,1)}), bf16[8,104,364]{2,1,0:T(8,128)(2,1)S(1)}, u32[]{:S(2)}, u32[]{:S(2)}) async-start(bf16[8,104,364]{2,1,0:T(8,128)(2,1)} %select_select_fusion.1), calls=%async_computation | async-start | bytes 1277952 | tf_op jit(solution)/shard_map/all_to_all | solution.py:73
  23.1 7.8 %all-to-all-done = bf16[8,104,364]{2,1,0:T(8,128)(2,1)S(1)} async-done(((bf16[8,104,364]{2,1,0:T(8,128)(2,1)}), bf16[8,104,364]{2,1,0:T(8,128)(2,1)S(1)}, u32[]{:S(2)}, u32[]{:S(2)}) %all-to-all-start) | async-done | bytes 605728 | tf_op jit(solution)/shard_map/all_to_all | solution.py:73
  30.9 3.0 gather_fusion.1
  34.3 2.2 gather_fusion.2
  36.7 1.1 select_select_fusion
  37.8 7.9 %all-to-all-start.1 = ((bf16[728,16,26]{0,2,1:T(8,128)(2,1)}), bf16[728,16,26]{0,2,1:T(8,128)(2,1)}, u32[]{:S(2)}, u32[]{:S(2)}) async-start(bf16[728,16,26]{0,2,1:T(8,128)(2,1)} %select_select_fusion), calls=%async_computation.1 | async-start | bytes 1572864 | tf_op jit(solution)/shard_map/all_to_all | solution.py:81
  46.1 4.7 %broadcast_in_dim.132 = f32[56,13,28,13]{1,0,3,2:T(8,128)} broadcast(f32[56,28]{0,1:T(8,128)S(1)} %convert_element_type.45), dimensions={0,2} | broadcast | bytes 1066240 | tf_op jit(solution)/shard_map/broadcast_in_dim | solution.py:86
  50.8 6.7 %reshape.386 = f32[728,364]{0,1:T(8,128)S(1)} reshape(f32[56,13,28,13]{1,0,3,2:T(8,128)} %broadcast_in_dim.132) | data formatting | bytes 2119936 | tf_op jit(solution)/shard_map/reshape | solution.py:88
  58.5 1.5 all_to_all.18
  60.0 2.2 gather_fusion.3
  63.4 7.5 %psum.28 = f32[]{:T(128)} all-reduce(f32[]{:T(128)} %fusion.5), channel_id=1, replica_groups=mesh['row_0'=4,'row_1'=2,'col_0'=4,'col_1'=4] {'row_0'}, use_global_device_ids=true, to_apply=%region_11.12 | all-reduce | flops 1 | bytes 8 | tf_op jit(solution)/shard_map/psum | solution.py:16
  70.8 7.3 %psum.29 = f32[]{:T(128)} all-reduce(f32[]{:T(128)} %psum.28), channel_id=1, replica_groups=mesh['row_0'=4,'row_1'=2,'col_0'=4,'col_1'=4] {'row_1'}, use_global_device_ids=true, to_apply=%region_12.13 | all-reduce | flops 1 | bytes 8 | tf_op jit(solution)/shard_map/psum | solution.py:16
  78.2 7.6 %psum.30 = f32[]{:T(128)} all-reduce(f32[]{:T(128)} %psum.29), channel_id=1, replica_groups=mesh['row_0'=4,'row_1'=2,'col_0'=4,'col_1'=4] {'col_0'}, use_global_device_ids=true, to_apply=%region_13.14 | all-reduce | flops 1 | bytes 8 | tf_op jit(solution)/shard_map/psum | solution.py:16
  85.8 9.0 %psum.31 = f32[]{:T(128)} all-reduce(f32[]{:T(128)} %psum.30), channel_id=1, replica_groups=mesh['row_0'=4,'row_1'=2,'col_0'=4,'col_1'=4] {'col_1'}, use_global_device_ids=true, to_apply=%region_14.15 | all-reduce | flops 1 | bytes 8 | tf_op jit(solution)/shard_map/psum | solution.py:16
  95.7 4.2 %stack.2 = bf16[16,728,364]{2,1,0:T(8,128)(2,1)} broadcast(bf16[728,364]{1,0:T(8,128)(2,1)S(1)} %fusion.7), dimensions={1,2} | broadcast | bytes 9009728 | tf_op jit(solution)/shard_map/stack | solution.py:93
  99.9 4.7 %all-to-all-start.2 = ((bf16[16,728,364]{2,1,0:T(8,128)(2,1)}), bf16[16,728,364]{2,1,0:T(8,128)(2,1)}, u32[]{:S(2)}, u32[]{:S(2)}) async-start(bf16[16,728,364]{2,1,0:T(8,128)(2,1)} %stack.2), calls=%async_computation.2 | async-start | bytes 17891328 | tf_op jit(solution)/shard_map/all_to_all | solution.py:93
  105.6 118.4 %all-to-all-done.2 = bf16[16,728,364]{2,1,0:T(8,128)(2,1)} async-done(((bf16[16,728,364]{2,1,0:T(8,128)(2,1)}), bf16[16,728,364]{2,1,0:T(8,128)(2,1)}, u32[]{:S(2)}, u32[]{:S(2)}) %all-to-all-start.2) | async-done | bytes 8479776 | tf_op jit(solution)/shard_map/all_to_all | solution.py:93
  224.0 8.1 %copy.34 = bf16[728,16,364]{2,1,0:T(8,128)(2,1)} copy(bf16[728,16,364]{2,0,1:T(8,128)(2,1)} %bitcast.6) | data formatting | bytes 16959488 | tf_op jit(solution)/shard_map/reshape | solution.py:92
  232.2 15.7 %reshape.388 = bf16[728,5824]{1,0:T(8,128)(2,1)} reshape(bf16[728,16,364]{2,1,0:T(8,128)(2,1)} %copy.34) | data formatting | bytes 16959488 | tf_op jit(solution)/shard_map/reshape | solution.py:92
  247.9 10.2 %fusion.3 = bf16[728,364]{1,0:T(8,128)(2,1)} fusion(f32[728,364]{1,0:T(8,128)S(1)} %copy.37, bf16[728,5824]{1,0:T(8,128)(2,1)} %reshape.388, bf16[5824,364]{1,0:T(8,128)(2,1)} %all-gather.3.cloned.1.call-done), kind=kOutput, calls=%fused_computation.9 | convolution fusion | flops 3087156736 | bytes 14309568 | tf_op jit(solution)/shard_map/dot_general | solution.py:44
  258.1 41.2 %all-gather.5.cloned.1.call-done = bf16[5824,364]{1,0:T(8,128)(2,1)} async-done(((bf16[728,364]{1,0:T(8,128)(2,1)}), bf16[5824,364]{1,0:T(8,128)(2,1)}) %all-gather.5.cloned.1.call-update) | async-done | bytes 4239888 | tf_op jit(solution)/shard_map/all_gather | solution.py:46
  299.3 10.4 %fusion.2 = f32[728,364]{1,0:T(8,128)} fusion(f32[728,364]{1,0:T(8,128)S(1)} %copy.37, bf16[728,5824]{1,0:T(8,128)(2,1)} %reshape.388, bf16[5824,364]{1,0:T(8,128)(2,1)} %all-gather.5.cloned.1.call-done, bf16[728,364]{1,0:T(8,128)(2,1)S(1)} %copy-done.3), kind=kOutput, calls=%fused_computation.8 | convolution fusion | flops 3088216576 | bytes 15369536 | tf_op jit(solution)/shard_map/dot_general | solution.py:44
  (96 shorter events, 10.3 us)
Async XLA Ops:
  6.5 3.2 %copy-start = (bf16[728,364]{1,0:T(8,128)(2,1)S(1)}, bf16[728,364]{1,0:T(8,128)(2,1)}, u32[]{:S(2)}) copy-start(bf16[728,364]{1,0:T(8,128)(2,1)} %param.3) | copy-start | bytes 1589956
  13.2 6.9 %copy-start.5 = (s32[448]{0:T(512)S(1)}, s32[448]{0:T(512)}, u32[]{:S(2)}) copy-start(s32[448]{0:T(512)} %param.4) | copy-start | bytes 5380
  14.4 16.5 %all-to-all-start = ((bf16[8,104,364]{2,1,0:T(8,128)(2,1)}), bf16[8,104,364]{2,1,0:T(8,128)(2,1)S(1)}, u32[]{:S(2)}, u32[]{:S(2)}) async-start(bf16[8,104,364]{2,1,0:T(8,128)(2,1)} %select_select_fusion.1), calls=%async_computation | async-start | bytes 1277952 | tf_op jit(solution)/shard_map/all_to_all | solution.py:73
  37.8 8.3 %copy-start.4 = (s32[56,28]{0,1:T(8,128)S(1)}, s32[56,28]{0,1:T(8,128)}, u32[]{:S(2)}) copy-start(s32[56,28]{0,1:T(8,128)} %param.5) | copy-start | bytes 18820
  37.8 20.8 %all-to-all-start.1 = ((bf16[728,16,26]{0,2,1:T(8,128)(2,1)}), bf16[728,16,26]{0,2,1:T(8,128)(2,1)}, u32[]{:S(2)}, u32[]{:S(2)}) async-start(bf16[728,16,26]{0,2,1:T(8,128)(2,1)} %select_select_fusion), calls=%async_computation.1 | async-start | bytes 1572864 | tf_op jit(solution)/shard_map/all_to_all | solution.py:81
  95.7 4.2 %copy-start.2 = (bf16[728,364]{1,0:T(8,128)(2,1)}, bf16[728,364]{1,0:T(8,128)(2,1)S(1)}, u32[]{:S(2)}) copy-start(bf16[728,364]{1,0:T(8,128)(2,1)S(1)} %fusion.7) | copy-start | bytes 1589956
  99.9 124.1 %all-to-all-start.2 = ((bf16[16,728,364]{2,1,0:T(8,128)(2,1)}), bf16[16,728,364]{2,1,0:T(8,128)(2,1)}, u32[]{:S(2)}, u32[]{:S(2)}) async-start(bf16[16,728,364]{2,1,0:T(8,128)(2,1)} %stack.2), calls=%async_computation.2 | async-start | bytes 17891328 | tf_op jit(solution)/shard_map/all_to_all | solution.py:93
  104.7 143.2 %all-gather.3.cloned.1.call-start = ((), (), s32[]{:S(2)}) async-start(), calls=%async_computation.3 | async-start | bytes 5031936 | tf_op jit(solution)/shard_map/all_gather | solution.py:46
  105.4 193.9 %all-gather.5.cloned.1.call-start = ((), (), s32[]{:S(2)}) async-start(), calls=%async_computation.4 | async-start | bytes 5031936 | tf_op jit(solution)/shard_map/all_gather | solution.py:46
  247.9 51.4 %copy-start.3 = (bf16[728,364]{1,0:T(8,128)(2,1)S(1)}, bf16[728,364]{1,0:T(8,128)(2,1)}, u32[]{:S(2)}) copy-start(bf16[728,364]{1,0:T(8,128)(2,1)} %copy-done.2) | copy-start | bytes 1589956
  299.3 10.4 %copy-start.1 = (bf16[728,364]{1,0:T(8,128)(2,1)S(1)}, bf16[728,364]{1,0:T(8,128)(2,1)}, u32[]{:S(2)}) copy-start(bf16[728,364]{1,0:T(8,128)(2,1)} %param.3) | copy-start | bytes 1589956
Sparse Core Ops, SparseCore 0:
  107.2 36.6 all-gather.2
  258.3 40.9 all-gather.4
